TPU v7x, 512 devices: a whole 4x4x16 slice. The times are simulated.
512 devices in a mesh: row: 32 (over x, y, core), col: 16 (over z).
Axes of the slice: x: 4, y: 4, z: 16, core: 2. Of those that a mesh axis runs over, the one named last changes fastest.
Arguments:
- tokens: bfloat16 [512, 12288], P('col', 'row'), may hold values from -6 to 6
- cotangent: bfloat16 [512, 12288], P('col', 'row'), may hold values from -1.5 to 1.5
- w_in: bfloat16 [12288, 24576], P('row', 'col'), may hold values from -0.0546875 to 0.0546875
- w_out: bfloat16 [24576, 12288], P('col', 'row'), may hold values from -0.0390625 to 0.0390625
Outputs:
- layer_out: bfloat16 [512, 12288], P('col', 'row')
- grad_tokens: bfloat16 [512, 12288], P('col', 'row')
- grad_w_in: bfloat16 [12288, 24576], P('row', 'col')
- grad_w_out: bfloat16 [24576, 12288], P('col', 'row')
All inputs are finite; a program needn't handle non-finite values.
Results may differ from a plain program's by a relative error of at most 0.034.
Values may be sent and summed in bfloat16 or wider, within the bound.
A program may use at most 64 MiB of HBM per device.

v0:
```python
import jax
import jax.numpy as jnp
from jax import lax
from jax.sharding import PartitionSpec as P


def gelu_fn(value):
    return jax.nn.gelu(value, approximate=True)


def gelu_back(hidden, grad_act):
    unused, pullback = jax.vjp(gelu_fn, hidden)
    return pullback(grad_act)[0].astype(jnp.bfloat16)


def shards(tokens, cotangent, w_in, w_out):
    token_full, cot_full = (
        lax.all_gather(tokens, "col", axis=0, tiled=True),
        lax.all_gather(cotangent, "col", axis=0, tiled=True),
    )
    block = token_full
    hidden_share = lax.psum_scatter(
        jnp.dot(block, w_in, preferred_element_type=jnp.float32).astype(jnp.bfloat16),
        "row",
        scatter_dimension=0,
        tiled=True,
    ).astype(jnp.float32)
    act_share = gelu_fn(hidden_share).astype(jnp.bfloat16)
    act = lax.all_gather(act_share, "row", axis=0, tiled=True)
    block = act
    layer_out = lax.psum_scatter(
        jnp.dot(block, w_out, preferred_element_type=jnp.float32).astype(jnp.bfloat16),
        "col",
        scatter_dimension=0,
        tiled=True,
    )
    block = cot_full
    grad_share = lax.psum_scatter(
        lax.dot_general(
            block, w_out, (((1,), (1,)), ((), ())), preferred_element_type=jnp.float32
        ).astype(jnp.bfloat16),
        "row",
        scatter_dimension=0,
        tiled=True,
    ).astype(jnp.float32)
    grad_hidden_share = gelu_back(hidden_share, grad_share)
    grad_hidden = lax.all_gather(grad_hidden_share, "row", axis=0, tiled=True)
    grad_w_out = lax.dot_general(
        act, cot_full, (((0,), (0,)), ((), ())), preferred_element_type=jnp.float32
    ).astype(jnp.bfloat16)
    grad_w_in = lax.dot_general(
        token_full, grad_hidden, (((0,), (0,)), ((), ())), preferred_element_type=jnp.float32
    ).astype(jnp.bfloat16)
    block = grad_hidden
    grad_tokens = lax.psum_scatter(
        lax.dot_general(
            block, w_in, (((1,), (1,)), ((), ())), preferred_element_type=jnp.float32
        ).astype(jnp.bfloat16),
        "col",
        scatter_dimension=0,
        tiled=True,
    )
    return (layer_out, grad_tokens, grad_w_in, grad_w_out)


def solution(mesh):
    return jax.shard_map(
        shards,
        mesh=mesh,
        in_specs=(P("col", "row"), P("col", "row"), P("row", "col"), P("col", "row")),
        out_specs=(P("col", "row"), P("col", "row"), P("row", "col"), P("col", "row")),
        check_vma=False,
    )
```

profile of v0, /device:TPU:6, one launch (start us, length us, event | category | flops | bytes accessed | tf_op | source)
XLA Modules:
  0.0 522.0 jit_solution(14763633044955557940)
XLA Ops:
  7.2 0.0 copy-start
  7.2 0.0 reduce-scatter.9.cloned.1.call-start
  7.2 38.2 %all_gather.14 = bf16[512,384]{1,0:T(8,128)(2,1)S(1)} all-gather(bf16[32,384]{1,0:T(8,128)(2,1)} %param.5), channel_id=1, replica_groups=mesh['row'=32,'col'=16] {'col'}, dimensions={0}, use_global_device_ids=true | all-gather | bytes 417792 | tf_op jit(solution)/shard_map/all_gather | solution.py:19
  45.5 0.0 copy-done
  45.5 2.2 convolution_convert_fusion
  47.6 0.0 reduce-scatter.9.cloned.1.call-update
  47.7 0.0 reduce-scatter.5.cloned.1.call-start
  47.7 0.7 copy-done.2
  48.4 28.2 %all_gather.12 = bf16[512,384]{1,0:T(8,128)(2,1)S(1)} all-gather(bf16[32,384]{1,0:T(8,128)(2,1)S(1)} %copy-done.2), channel_id=1, replica_groups=mesh['row'=32,'col'=16] {'col'}, dimensions={0}, use_global_device_ids=true | all-gather | bytes 417792 | tf_op jit(solution)/shard_map/all_gather | solution.py:18
  76.6 0.0 copy-done.1
  76.6 2.1 convolution_convert_fusion.1
  78.8 0.0 reduce-scatter.5.cloned.1.call-update
  78.8 0.0 all-gather.3.cloned.1.call-start
  78.8 65.7 %reduce-scatter.9.cloned.1.call-done = bf16[16,1536]{1,0:T(8,128)(2,1)} async-done(((bf16[512,1536]{1,0:T(8,128)(2,1)}), bf16[16,1536]{1,0:T(8,128)(2,1)}) %reduce-scatter.9.cloned.1.call-update) | async-done | bytes 49168 | tf_op jit(solution)/shard_map/reduce_scatter | solution.py:38
  144.5 105.2 %reduce-scatter.5.cloned.1.call-done = bf16[16,1536]{1,0:T(8,128)(2,1)} async-done(((bf16[512,1536]{1,0:T(8,128)(2,1)}), bf16[16,1536]{1,0:T(8,128)(2,1)}) %reduce-scatter.5.cloned.1.call-update) | async-done | bytes 49168 | tf_op jit(solution)/shard_map/reduce_scatter | solution.py:22
  249.6 1.5 fusion.4
  251.2 0.0 all-gather.3.cloned.1.call-update
  251.2 0.0 all-gather.5.cloned.1.call-start
  251.3 0.5 all-gather.5.cloned.1.call-update
  251.8 0.0 reduce-scatter.7.cloned.1.call-start
  251.8 59.5 %all-gather.3.cloned.1.call-done = bf16[512,1536]{1,0:T(8,128)(2,1)} async-done(((bf16[16,1536]{1,0:T(8,128)(2,1)}), bf16[512,1536]{1,0:T(8,128)(2,1)}) %all-gather.3.cloned.1.call-update) | async-done | bytes 1572880 | tf_op jit(solution)/shard_map/all_gather | solution.py:29
  311.4 3.1 convolution_convert_fusion.5
  314.5 0.0 reduce-scatter.7.cloned.1.call-update
  314.5 0.0 reduce-scatter.11.cloned.1.call-start
  314.6 58.4 %all-gather.5.cloned.1.call-done = bf16[512,1536]{1,0:T(8,128)(2,1)} async-done(((bf16[16,1536]{1,0:T(8,128)(2,1)}), bf16[512,1536]{1,0:T(8,128)(2,1)}) %all-gather.5.cloned.1.call-update) | async-done | bytes 1572880 | tf_op jit(solution)/shard_map/all_gather | solution.py:47
  373.0 3.2 convolution_convert_fusion.4
  376.1 0.0 reduce-scatter.11.cloned.1.call-update
  376.2 2.4 fusion
  378.6 1.5 copy.8
  380.0 3.4 convolution_convert_fusion.2
  383.5 61.5 %reduce-scatter.7.cloned.1.call-done = bf16[32,384]{1,0:T(8,128)(2,1)} async-done(((bf16[512,384]{1,0:T(8,128)(2,1)}), bf16[32,384]{1,0:T(8,128)(2,1)}) %reduce-scatter.7.cloned.1.call-update) | async-done | bytes 24592 | tf_op jit(solution)/shard_map/reduce_scatter | solution.py:31
  444.9 70.2 %reduce-scatter.11.cloned.1.call-done = bf16[32,384]{1,0:T(8,128)(2,1)} async-done(((bf16[512,384]{1,0:T(8,128)(2,1)}), bf16[32,384]{1,0:T(8,128)(2,1)}) %reduce-scatter.11.cloned.1.call-update) | async-done | bytes 24592 | tf_op jit(solution)/shard_map/reduce_scatter | solution.py:55
  (2 shorter events, 0.0 us)
Async XLA Ops:
  7.2 38.3 %copy-start = (bf16[1536,384]{1,0:T(8,128)(2,1)S(1)}, bf16[1536,384]{1,0:T(8,128)(2,1)}, u32[]{:S(2)}) copy-start(bf16[1536,384]{1,0:T(8,128)(2,1)} %param.7) | copy-start | bytes 3538948
  7.2 137.3 %reduce-scatter.9.cloned.1.call-start = ((), (), s32[]{:S(2)}) async-start(), calls=%async_computation.7 | async-start | bytes 1622016 | tf_op jit(solution)/shard_map/reduce_scatter | solution.py:38
  47.6 0.7 copy-start.2
  47.6 29.0 %copy-start.1 = (bf16[384,1536]{1,0:T(8,128)(2,1)S(1)}, bf16[384,1536]{1,0:T(8,128)(2,1)}, u32[]{:S(2)}) copy-start(bf16[384,1536]{1,0:T(8,128)(2,1)} %param.6) | copy-start | bytes 3538948
  47.7 202.0 %reduce-scatter.5.cloned.1.call-start = ((), (), s32[]{:S(2)}) async-start(), calls=%async_computation.4 | async-start | bytes 1622016 | tf_op jit(solution)/shard_map/reduce_scatter | solution.py:22
  78.8 232.6 %all-gather.3.cloned.1.call-start = ((), (), s32[]{:S(2)}) async-start(), calls=%async_computation.5 | async-start | bytes 1622016 | tf_op jit(solution)/shard_map/all_gather | solution.py:29
  251.2 121.7 %all-gather.5.cloned.1.call-start = ((), (), s32[]{:S(2)}) async-start(), calls=%async_computation.8 | async-start | bytes 1622016 | tf_op jit(solution)/shard_map/all_gather | solution.py:47
  251.8 193.2 %reduce-scatter.7.cloned.1.call-start = ((), (), s32[]{:S(2)}) async-start(), calls=%async_computation.6 | async-start | bytes 417792 | tf_op jit(solution)/shard_map/reduce_scatter | solution.py:31
  314.5 200.6 %reduce-scatter.11.cloned.1.call-start = ((), (), s32[]{:S(2)}) async-start(), calls=%async_computation.9 | async-start | bytes 417792 | tf_op jit(solution)/shard_map/reduce_scatter | solution.py:55
Sparse Core Ops, SparseCore 0:
  47.8 96.6 reduce-scatter.8
  148.9 100.6 reduce-scatter.4
  253.4 57.9 all-gather.2
  314.9 57.9 all-gather.4
  376.2 68.7 reduce-scatter.6
  448.4 66.7 reduce-scatter.10
where the time goes:
time: 522 us
  waiting for transfers between devices  421 us (81%)
  blocking collectives  66.5 us (13%)
  matrix products  16.5 us (3%)
  between operations  14.1 us (3%)
    reduce_scatter x1, waiting for transfers between devices, shards(): lax.psum_scatter(jnp.dot(block, w_in, preferred_element_type=jnp.float32)...  105 us
    reduce_scatter x1, waiting for transfers between devices, shards(): lax.psum_scatter(lax.dot_general(block, w_in, (((1,), (1,)), ((), ())), p...  70.2 us
    reduce_scatter x1, waiting for transfers between devices, shards(): lax.psum_scatter(lax.dot_general(block, w_out, (((1,), (1,)), ((), ())),...  65.7 us
    reduce_scatter x1, waiting for transfers between devices, shards(): lax.psum_scatter(jnp.dot(block, w_out, preferred_element_type=jnp.float32...  61.5 us
    all_gather x1, waiting for transfers between devices, shards(): act = lax.all_gather(act_share, 'row', axis=0, tiled=True)  59.5 us
    all_gather x1, waiting for transfers between devices, shards(): grad_hidden = lax.all_gather(grad_hidden_share, 'row', axis=0, tiled=True)  58.4 us
    all_gather x1, blocking collectives, shards(): lax.all_gather(cotangent, 'col', axis=0, tiled=True)  38.2 us
    all_gather x1, blocking collectives, shards(): lax.all_gather(tokens, 'col', axis=0, tiled=True)  28.2 us
  transfers between devices with their start and end apart: 6, of which 6 were waited for; matrix products, arithmetic and copies ran while one was open for 3% of the time, Pallas kernels for 0%

commit v1 on v0

v1 whole, which is shorter than its diff:
```python
import functools
import math

import jax
import jax.numpy as jnp
from jax import lax
from jax.experimental import pallas as pl
from jax.experimental.pallas import tpu as pltpu
from jax.sharding import PartitionSpec as P

MESH = pl.DeviceIdType.MESH
BF16, F32 = jnp.bfloat16, jnp.float32
NZ = 16
CHUNK = 32
TOKENS = NZ * CHUNK
W = 384
CW = 2 * W
H = 1536
HH = H // 2
GROUPS = 2
ROWS = TOKENS // GROUPS
PART = ROWS // 4
PIECE = PART // 4
ORDER = [0, 15, 1, 14, 2, 13, 3, 12, 4, 11, 5, 10, 6, 9, 7, 8]
PLACE = {slot: place for place, slot in enumerate(ORDER)}
K0, K1 = math.sqrt(2.0 / math.pi), 0.044715


def chunk_rows(direction, steps):
    return pl.ds(PLACE[(-direction * steps) % NZ] * CHUNK, CHUNK)


def reach(which, direction):
    return 8 if (direction == 1) == (which == 0) else 7


def body(
    tokens, cotangent, w_in, w_out,
    layer_out, grad_tokens, grad_w_in, grad_w_out,
    ins, wi, wo, wi_pair, wo_pair, share, got1, mid, got2, full, part, zgot, zsum, outs, gwi, gwo,
    local_sem, send_sem, recv_sem,
):
    row, z = lax.axis_index("row"), lax.axis_index("col")
    x, y, c = row // 8, (row // 2) % 4, row % 2
    other = 1 - c
    own_cols = pl.ds(pl.multiple_of(c * W, 128), W)

    def along(axis, step):
        if axis == "x":
            return (((x + step) % 4) * 8 + y * 2 + c, z)
        if axis == "y":
            return (x * 8 + ((y + step) % 4) * 2 + c, z)
        return (row, (z + step + NZ) % NZ)

    pair = (x * 8 + y * 2 + other, z)
    at = {"x": x, "y": y}

    locals_, copies = [], {}

    def local(source, target):
        copy = pltpu.make_async_copy(source, target, local_sem.at[len(locals_)])
        copy.start()
        locals_.append(copy)
        return copy

    def send(key, source, target, device):
        index = len(copies)
        copies[key] = copy = pltpu.make_async_remote_copy(
            src_ref=source, dst_ref=target, send_sem=send_sem.at[index], recv_sem=recv_sem.at[index],
            device_id=device, device_id_type=MESH,
        )
        copy.start()

    def arrived(*key):
        copies[key].wait_recv()

    mine = [local(ref, ins.at[i, pl.ds(0, CHUNK), own_cols]) for i, ref in enumerate((tokens, cotangent))]
    barrier = pltpu.get_barrier_semaphore()
    partners = [along("x", s) for s in (1, 2, 3)] + [along("y", s) for s in (1, 2, 3)]
    partners += [along("z", s) for s in (-2, -1, 1, 2)] + [pair]
    for device in partners:
        pl.semaphore_signal(barrier, inc=1, device_id=device, device_id_type=MESH)
    own_weights = [
        local(w_in.at[:, pl.ds(pl.multiple_of(c * HH, 128), HH)], wi_pair.at[pl.ds(pl.multiple_of(c * W, 128), W)]),
        local(w_out.at[pl.ds(pl.multiple_of(c * HH, 128), HH)], wo_pair.at[:, own_cols]),
        local(w_in, wi),
        local(w_out, wo),
    ]
    pl.semaphore_wait(barrier, len(partners))
    for copy in mine:
        copy.wait()

    def pass_on(which, direction, steps):
        rows = chunk_rows(direction, steps)
        if steps % 2 == 0:
            for hop in (2, 1):
                if steps + hop <= reach(which, direction):
                    send(
                        ("gather", which, direction, steps + hop), ins.at[which, rows, own_cols],
                        ins.at[which, chunk_rows(direction, steps + hop), own_cols], along("z", direction * hop),
                    )

    def to_pair(which, direction, steps):
        rows = chunk_rows(direction, steps)
        key = ("pair", which, direction, steps)
        send(key, ins.at[which, rows, own_cols], ins.at[which, rows, own_cols], pair)

    def gather_step(steps):
        for which in range(2):
            for direction in (1, -1):
                if steps <= reach(which, direction):
                    arrived("gather", which, direction, steps)
                    pass_on(which, direction, steps)
                    to_pair(which, direction, steps)

    def pair_has(which, group):
        for place in range(8 * group, 8 * group + 8):
            slot = ORDER[place]
            if slot == 0:
                arrived("pair", which, 1, 0)
            elif slot == 8:
                arrived("pair", which, 1 if which == 0 else -1, 8)
            else:
                arrived("pair", which, *((-1, slot) if slot < 8 else (1, 16 - slot)))

    def group_rows(group, begin=0, count=ROWS):
        return pl.ds(group * ROWS + begin, count)

    def product(which, group):
        block = ins[which, group_rows(group), :]
        if which == 0:
            value = jnp.dot(block, wi_pair[...], preferred_element_type=F32)
        else:
            value = lax.dot_general(block, wo_pair[...], (((1,), (1,)), ((), ())), preferred_element_type=F32)
        share[which, group_rows(group), :] = value.astype(BF16)

    def axes(half):
        return ("x", "y") if half == 0 else ("y", "x")

    def cols(half):
        return pl.ds(half * W, W)

    def part_at(group, index):
        return pl.ds(pl.multiple_of(group * ROWS + index * PART, 16), PART)

    def piece_at(group, half):
        first, second = (at[a] for a in axes(half))
        return pl.ds(pl.multiple_of(group * ROWS + first * PART + second * PIECE, 16), PIECE)

    def scatter1(which, group):
        for step in (2, 1, 3):
            for half in range(2):
                axis = axes(half)[0]
                target = (at[axis] + step) % 4
                send(
                    ("s1", which, group, half, step), share.at[which, part_at(group, target), cols(half)],
                    got1.at[which, group, half, step - 1], along(axis, step),
                )

    def scatter2(which, group):
        for half in range(2):
            first, second = axes(half)
            total = share[which, part_at(group, at[first]), cols(half)].astype(F32)
            for step in (1, 3, 2):
                arrived("s1", which, group, half, step)
                total += got1[which, group, half, step - 1].astype(F32)
            mid[which, group, half] = total.astype(BF16)
            for step in (2, 1, 3):
                target = (at[second] + step) % 4
                send(
                    ("s2", which, group, half, step),
                    mid.at[which, group, half, pl.ds(pl.multiple_of(target * PIECE, 16), PIECE)],
                    got2.at[which, group, half, step - 1], along(second, step),
                )

    hidden = {}

    def finish(which, group):
        for half in range(2):
            second = axes(half)[1]
            total = mid[which, group, half, pl.ds(pl.multiple_of(at[second] * PIECE, 16), PIECE)].astype(F32)
            for step in (1, 3, 2):
                arrived("s2", which, group, half, step)
                total += got2[which, group, half, step - 1].astype(F32)
            if which == 0:
                hidden[group, half] = total
            v = hidden[group, half]
            t = jnp.tanh(K0 * (v + K1 * (v * v * v)))
            if which == 0:
                value = 0.5 * v * (1.0 + t)
            else:
                slope = 0.5 * (1.0 + t) + 0.5 * v * (1.0 - t * t) * (K0 * (1.0 + 3.0 * K1 * (v * v)))
                value = total * slope
            place = (which, c, piece_at(group, half), cols(half))
            full[place] = value.astype(BF16)
            for step in (2, 1, 3):
                send(("g1", which, group, half, step), full.at[place], full.at[place], along(second, step))

    def gather2(which, group):
        for half in range(2):
            first, second = axes(half)
            for step in (1, 3, 2):
                arrived("g1", which, group, half, step)
            place = (which, c, part_at(group, at[first]), cols(half))
            for step in (2, 1, 3):
                send(("g2", which, group, half, step), full.at[place], full.at[place], along(first, step))
            send(("gp", which, group, half, 0), full.at[place], full.at[place], pair)

    def gather3(which, group):
        for step in (1, 3, 2):
            for half in range(2):
                first = axes(half)[0]
                arrived("g2", which, group, half, step)
                place = (which, c, part_at(group, (at[first] + 4 - step) % 4), cols(half))
                send(("gp", which, group, half, step), full.at[place], full.at[place], pair)

    def project(which, group):
        for half in range(2):
            for step in range(4):
                arrived("gp", which, group, half, step)
        value = None
        for k in range(2):
            block = full[which, k, group_rows(group), :]
            if which == 0:
                term = jnp.dot(block, wo[pl.ds(k * HH, HH), :], preferred_element_type=F32)
            else:
                term = lax.dot_general(
                    block, wi[:, pl.ds(k * HH, HH)], (((1,), (1,)), ((), ())), preferred_element_type=F32
                )
            value = term if value is None else value + term
        part[which, group_rows(group), :] = value.astype(BF16)

    def zsend(which, direction, steps, source):
        hop = 1 if steps % 2 else 2
        send(
            ("z", which, direction, steps), source,
            zgot.at[which, 0 if direction == 1 else 1, (steps - hop) // 2, hop - 1], along("z", -direction * hop),
        )

    def zraw(which, group):
        for direction in (1, -1):
            for steps in (8, 7, 5, 3, 1):
                slot = (-direction * steps) % NZ
                if steps <= reach(which, direction) and PLACE[slot] // 8 == group:
                    zsend(which, direction, steps, part.at[which, chunk_rows(direction, steps)])

    def zadd(which, direction, steps, total):
        for hop in (1, 2):
            if steps + hop <= reach(which, direction):
                arrived("z", which, direction, steps + hop)
                total += zgot[which, 0 if direction == 1 else 1, steps // 2, hop - 1].astype(F32)
        return total

    def zstep(which, steps):
        for side, direction in enumerate((1, -1)):
            total = part[which, chunk_rows(direction, steps), :].astype(F32)
            zsum[which, side, steps // 2 - 1] = zadd(which, direction, steps, total).astype(BF16)
            zsend(which, direction, steps, zsum.at[which, side, steps // 2 - 1])

    def zend(which):
        total = part[which, chunk_rows(1, 0), :].astype(F32)
        for direction in (1, -1):
            total = zadd(which, direction, 0, total)
        outs[which] = total.astype(BF16)
        return local(outs.at[which], (layer_out, grad_tokens)[which])

    def weight_grad(which):
        own = ins[1 - which, :, own_cols]
        for k in range(2):
            if which == 0:
                value = lax.dot_general(full[0, k], own, (((0,), (0,)), ((), ())), preferred_element_type=F32)
                gwo[pl.ds(k * HH, HH), :] = value.astype(BF16)
            else:
                value = lax.dot_general(own, full[1, k], (((0,), (0,)), ((), ())), preferred_element_type=F32)
                gwi[:, pl.ds(k * HH, HH)] = value.astype(BF16)
        return local(gwo, grad_w_out) if which == 0 else local(gwi, grad_w_in)

    for hop in (2, 1):
        for which in range(2):
            for direction in (1, -1):
                send(
                    ("gather", which, direction, hop), ins.at[which, chunk_rows(1, 0), own_cols],
                    ins.at[which, chunk_rows(direction, hop), own_cols], along("z", direction * hop),
                )
    for which in range(2):
        to_pair(which, 1, 0)
    own_half, other_half = (pl.ds(pl.multiple_of(i * HH, 128), HH) for i in (c, other))
    send(("w", 0), w_in.at[:, other_half], wi_pair.at[pl.ds(pl.multiple_of(c * W, 128), W)], pair)
    send(("w", 1), w_out.at[other_half], wo_pair.at[:, own_cols], pair)

    for steps in (2, 1, 4, 3):
        gather_step(steps)
    for copy in own_weights:
        copy.wait()
    arrived("w", 0)
    pair_has(0, 0)
    product(0, 0)
    scatter1(0, 0)
    gather_step(6)
    arrived("w", 1)
    pair_has(1, 0)
    product(1, 0)
    scatter1(1, 0)
    gather_step(5)
    gather_step(8)
    gather_step(7)
    scatter2(0, 0)
    pair_has(0, 1)
    product(0, 1)
    scatter1(0, 1)
    scatter2(1, 0)
    pair_has(1, 1)
    product(1, 1)
    scatter1(1, 1)
    finish(0, 0)
    finish(1, 0)
    scatter2(0, 1)
    gather2(0, 0)
    scatter2(1, 1)
    gather2(1, 0)
    finish(0, 1)
    finish(1, 1)
    gather3(0, 0)
    gather2(0, 1)
    gather2(1, 1)
    gather3(1, 0)
    project(0, 0)
    zraw(0, 0)
    gather3(0, 1)
    project(1, 0)
    zraw(1, 0)
    project(0, 1)
    zraw(0, 1)
    gather3(1, 1)
    project(1, 1)
    zraw(1, 1)
    zstep(0, 6)
    zstep(1, 6)
    last = [weight_grad(0)]
    zstep(0, 4)
    zstep(1, 4)
    last.append(weight_grad(1))
    zstep(0, 2)
    zstep(1, 2)
    last.append(zend(0))
    last.append(zend(1))
    for copy in copies.values():
        copy.wait_send()
    for copy in last:
        copy.wait()


def shards(tokens, cotangent, w_in, w_out):
    copies = 2 * 15 + 2 * 16 + 2 + 4 * 6 * 4 + 4 * 8 + 2 * 15
    anywhere = pl.BlockSpec(memory_space=pl.ANY)
    shape = jax.ShapeDtypeStruct
    return pl.pallas_call(
        body,
        out_shape=(
            shape((CHUNK, W), BF16), shape((CHUNK, W), BF16), shape((W, H), BF16), shape((H, W), BF16),
        ),
        in_specs=[anywhere] * 4,
        out_specs=(anywhere,) * 4,
        scratch_shapes=[
            pltpu.VMEM((2, TOKENS, CW), BF16),
            pltpu.VMEM((W, H), BF16),
            pltpu.VMEM((H, W), BF16),
            pltpu.VMEM((CW, HH), BF16),
            pltpu.VMEM((HH, CW), BF16),
            pltpu.VMEM((2, TOKENS, HH), BF16),
            pltpu.VMEM((2, GROUPS, 2, 3, PART, W), BF16),
            pltpu.VMEM((2, GROUPS, 2, PART, W), BF16),
            pltpu.VMEM((2, GROUPS, 2, 3, PIECE, W), BF16),
            pltpu.VMEM((2, 2, TOKENS, HH), BF16),
            pltpu.VMEM((2, TOKENS, W), BF16),
            pltpu.VMEM((2, 2, 4, 2, CHUNK, W), BF16),
            pltpu.VMEM((2, 2, 3, CHUNK, W), BF16),
            pltpu.VMEM((2, CHUNK, W), BF16),
            pltpu.VMEM((W, H), BF16),
            pltpu.VMEM((H, W), BF16),
            pltpu.SemaphoreType.DMA((10,)),
            pltpu.SemaphoreType.DMA((copies,)),
            pltpu.SemaphoreType.DMA((copies,)),
        ],
        compiler_params=pltpu.CompilerParams(
            collective_id=0, has_side_effects=True, vmem_limit_bytes=48 * 2**20
        ),
        cost_estimate=pl.CostEstimate(flops=12 * TOKENS * W * H, bytes_accessed=10 * W * H, transcendentals=0),
        name="ffn",
    )(tokens, cotangent, w_in, w_out)


def solution(mesh):
    return jax.shard_map(
        shards,
        mesh=mesh,
        in_specs=(P("col", "row"), P("col", "row"), P("row", "col"), P("col", "row")),
        out_specs=(P("col", "row"), P("col", "row"), P("row", "col"), P("col", "row")),
        check_vma=False,
    )
```

time: 522 us -> 85.3 us (0.16)
  waiting for transfers between devices: 421 us -> 0 us
  Pallas kernels: 0 us -> 77.1 us
  blocking collectives: 66.5 us -> 0 us
  matrix products: 16.5 us -> 0 us
  between operations: 14.1 us -> 0.65 us
    reduce_scatter x4 -> x0, waiting for transfers between devices: 303 us -> none  [the longest x1 105 us: shards(): lax.psum_scatter(jnp.dot(block, w_in, preferred_element_type=jnp.float32)...]
    all_gather x2 -> x0, waiting for transfers between devices: 118 us -> none  [the longest x1 59.5 us: shards(): act = lax.all_gather(act_share, 'row', axis=0, tiled=True)]
    pallas_call x0 -> x1, Pallas kernels: none -> 77.1 us  [shards(): pl.pallas_call(body, out_shape=(shape((CHUNK, W), BF16), shape((CHUNK, W)...]
    all_gather x2 -> x0, blocking collectives: 66.5 us -> none  [the longest x1 38.2 us: shards(): lax.all_gather(cotangent, 'col', axis=0, tiled=True)]
    dot_general x6 -> x0, matrix products: 16.5 us -> none  [the longest x1 3.43 us: shards(): lax.dot_general(act, cot_full, (((0,), (0,)), ((), ())), preferred_elemen...]
  transfers between devices with their start and end apart: 6 -> 0, of which waited for: 6 -> 0; matrix products, arithmetic and copies ran while one was open for 3% -> 0% of each run, Pallas kernels for 0% -> 0%
where the time goes in v1:
time: 85.3 us; the launch traced here: 85 us
  Pallas kernels  77.1 us (90%)
  local copies, waits for them, and re-layouts  7.25 us (8%)
    pallas_call x1, Pallas kernels, shards(): pl.pallas_call(body, out_shape=(shape((CHUNK, W), BF16), shape((CHUNK, W)...  77.1 us
    unnamed x12, local copies, waits for them, and re-layouts  7.25 us

profile of v1, /device:TPU:6, one launch (start us, length us, event | category | flops | bytes accessed | tf_op | source)
XLA Modules:
  0.0 85.0 jit_solution(12667644669995957766)
XLA Ops:
  0.6 0.0 copy-start
  0.6 1.3 %copy-done = bf16[384,1536]{1,0:T(8,128)(2,1)S(1)} copy-done((bf16[384,1536]{1,0:T(8,128)(2,1)S(1)}, bf16[384,1536]{1,0:T(8,128)(2,1)}, u32[]{:S(2)}) %copy-start) | copy-done | bytes 1179672
  1.9 0.0 copy-start.1
  1.9 1.3 %copy-done.1 = bf16[1536,384]{1,0:T(8,128)(2,1)S(1)} copy-done((bf16[1536,384]{1,0:T(8,128)(2,1)S(1)}, bf16[1536,384]{1,0:T(8,128)(2,1)}, u32[]{:S(2)}) %copy-start.1) | copy-done | bytes 1179672
  3.2 0.0 copy-start.2
  3.2 0.7 copy-done.2
  3.9 0.0 copy-start.3
  3.9 0.7 copy-done.3
  4.7 77.1 %ffn.1 = (bf16[32,384]{1,0:T(8,128)(2,1)S(1)}, bf16[32,384]{1,0:T(8,128)(2,1)S(1)}, bf16[384,1536]{1,0:T(8,128)(2,1)S(1)}, bf16[1536,384]{1,0:T(8,128)(2,1)S(1)}) custom-call(bf16[32,384]{1,0:T(8,128)(2,1)S(1)} %copy-done.2, bf16[32,384]{1,0:T(8,128)(2,1)S(1)} %copy-done.3, bf16[384,1536]{1,0:T(8,128)(2,1)S(1)} %copy-done, bf16[1536,384]{1,0:T(8,128)(2,1)S(1)} %copy-done.1), custom_call_target="tpu_custom_call" | custom-call | flops 3623878656 | bytes 5898240 | tf_op jit(solution)/shard_map/ffn/pallas_call | solution.py:357
  81.7 0.6 copy.12
  82.3 0.6 copy.13
  82.9 1.0 %copy.14 = bf16[384,1536]{1,0:T(8,128)(2,1)} copy(bf16[384,1536]{1,0:T(8,128)(2,1)S(1)} %get-tuple-element.10) | data formatting | bytes 2359296
  83.9 1.0 %copy.15 = bf16[1536,384]{1,0:T(8,128)(2,1)} copy(bf16[1536,384]{1,0:T(8,128)(2,1)S(1)} %get-tuple-element.11) | data formatting | bytes 2359296
Async XLA Ops:
  0.6 1.3 %copy-start = (bf16[384,1536]{1,0:T(8,128)(2,1)S(1)}, bf16[384,1536]{1,0:T(8,128)(2,1)}, u32[]{:S(2)}) copy-start(bf16[384,1536]{1,0:T(8,128)(2,1)} %w_in.1) | copy-start | bytes 3538948
  1.9 1.3 %copy-start.1 = (bf16[1536,384]{1,0:T(8,128)(2,1)S(1)}, bf16[1536,384]{1,0:T(8,128)(2,1)}, u32[]{:S(2)}) copy-start(bf16[1536,384]{1,0:T(8,128)(2,1)} %w_out.1) | copy-start | bytes 3538948
  3.2 0.7 copy-start.2
  3.9 0.7 copy-start.3

commit v2 on v1

--- a/solution.py
+++ b/solution.py
@@ -18,11 +18,15 @@
 H = 1536
 HH = H // 2
 GROUPS = 2
+SPAN = NZ // GROUPS
 ROWS = TOKENS // GROUPS
 PART = ROWS // 4
 PIECE = PART // 4
 ORDER = [0, 15, 1, 14, 2, 13, 3, 12, 4, 11, 5, 10, 6, 9, 7, 8]
 PLACE = {slot: place for place, slot in enumerate(ORDER)}
+GO_ON = {1: 0, 2: 0, 3: 2, 4: 2, 5: 4, 6: 4, 7: 6, 8: 6}
+BEFORE = {1: 0, 2: 0, 3: 0, 4: 3, 5: 3, 6: 3, 7: 6, 8: 6}
+FIRST = [steps for steps in (3, 2, 1) if GO_ON[steps] == 0]
 K0, K1 = math.sqrt(2.0 / math.pi), 0.044715
 
 
@@ -74,47 +78,52 @@
     def arrived(*key):
         copies[key].wait_recv()
 
+    gone = set()
+
+    def sent():
+        for key, copy in copies.items():
+            if key not in gone:
+                copy.wait_send()
+                gone.add(key)
+
     mine = [local(ref, ins.at[i, pl.ds(0, CHUNK), own_cols]) for i, ref in enumerate((tokens, cotangent))]
     barrier = pltpu.get_barrier_semaphore()
     partners = [along("x", s) for s in (1, 2, 3)] + [along("y", s) for s in (1, 2, 3)]
-    partners += [along("z", s) for s in (-2, -1, 1, 2)] + [pair]
+    partners += [along("z", s) for s in (-3, -2, -1, 1, 2, 3)] + [pair]
     for device in partners:
         pl.semaphore_signal(barrier, inc=1, device_id=device, device_id_type=MESH)
-    own_weights = [
-        local(w_in.at[:, pl.ds(pl.multiple_of(c * HH, 128), HH)], wi_pair.at[pl.ds(pl.multiple_of(c * W, 128), W)]),
-        local(w_out.at[pl.ds(pl.multiple_of(c * HH, 128), HH)], wo_pair.at[:, own_cols]),
-        local(w_in, wi),
-        local(w_out, wo),
-    ]
     pl.semaphore_wait(barrier, len(partners))
     for copy in mine:
         copy.wait()
 
-    def pass_on(which, direction, steps):
-        rows = chunk_rows(direction, steps)
-        if steps % 2 == 0:
-            for hop in (2, 1):
-                if steps + hop <= reach(which, direction):
-                    send(
-                        ("gather", which, direction, steps + hop), ins.at[which, rows, own_cols],
-                        ins.at[which, chunk_rows(direction, steps + hop), own_cols], along("z", direction * hop),
-                    )
+    def pass_on(which, steps):
+        for direction in (1, -1):
+            if steps <= reach(which, direction):
+                source, hop = GO_ON[steps], steps - GO_ON[steps]
+                send(
+                    ("gather", which, direction, steps), ins.at[which, chunk_rows(direction, source), own_cols],
+                    ins.at[which, chunk_rows(direction, steps), own_cols], along("z", direction * hop),
+                )
 
     def to_pair(which, direction, steps):
         rows = chunk_rows(direction, steps)
         key = ("pair", which, direction, steps)
         send(key, ins.at[which, rows, own_cols], ins.at[which, rows, own_cols], pair)
 
-    def gather_step(steps):
-        for which in range(2):
+    def chunk_in(which, *many):
+        for steps in many:
             for direction in (1, -1):
                 if steps <= reach(which, direction):
                     arrived("gather", which, direction, steps)
-                    pass_on(which, direction, steps)
+
+    def share_in(which, *many):
+        for steps in many:
+            for direction in (1, -1):
+                if steps <= reach(which, direction):
                     to_pair(which, direction, steps)
 
     def pair_has(which, group):
-        for place in range(8 * group, 8 * group + 8):
+        for place in range(SPAN * group, SPAN * group + SPAN):
             slot = ORDER[place]
             if slot == 0:
                 arrived("pair", which, 1, 0)
@@ -231,31 +240,32 @@
         part[which, group_rows(group), :] = value.astype(BF16)
 
     def zsend(which, direction, steps, source):
-        hop = 1 if steps % 2 else 2
+        after = BEFORE[steps]
         send(
             ("z", which, direction, steps), source,
-            zgot.at[which, 0 if direction == 1 else 1, (steps - hop) // 2, hop - 1], along("z", -direction * hop),
+            zgot.at[which, 0 if direction == 1 else 1, after // 3, steps - after - 1],
+            along("z", -direction * (steps - after)),
         )
 
     def zraw(which, group):
-        for direction in (1, -1):
-            for steps in (8, 7, 5, 3, 1):
+        for steps in (8, 7, 5, 4, 2, 1):
+            for direction in (1, -1):
                 slot = (-direction * steps) % NZ
-                if steps <= reach(which, direction) and PLACE[slot] // 8 == group:
+                if steps <= reach(which, direction) and PLACE[slot] // SPAN == group:
                     zsend(which, direction, steps, part.at[which, chunk_rows(direction, steps)])
 
     def zadd(which, direction, steps, total):
-        for hop in (1, 2):
-            if steps + hop <= reach(which, direction):
-                arrived("z", which, direction, steps + hop)
-                total += zgot[which, 0 if direction == 1 else 1, steps // 2, hop - 1].astype(F32)
+        for source in (steps + 1, steps + 2, steps + 3):
+            if source <= reach(which, direction) and BEFORE[source] == steps:
+                arrived("z", which, direction, source)
+                total += zgot[which, 0 if direction == 1 else 1, steps // 3, source - steps - 1].astype(F32)
         return total
 
     def zstep(which, steps):
         for side, direction in enumerate((1, -1)):
             total = part[which, chunk_rows(direction, steps), :].astype(F32)
-            zsum[which, side, steps // 2 - 1] = zadd(which, direction, steps, total).astype(BF16)
-            zsend(which, direction, steps, zsum.at[which, side, steps // 2 - 1])
+            zsum[which, side, steps // 3 - 1] = zadd(which, direction, steps, total).astype(BF16)
+            zsend(which, direction, steps, zsum.at[which, side, steps // 3 - 1])
 
     def zend(which):
         total = part[which, chunk_rows(1, 0), :].astype(F32)
@@ -275,35 +285,75 @@
                 gwi[:, pl.ds(k * HH, HH)] = value.astype(BF16)
         return local(gwo, grad_w_out) if which == 0 else local(gwi, grad_w_in)
 
-    for hop in (2, 1):
-        for which in range(2):
-            for direction in (1, -1):
-                send(
-                    ("gather", which, direction, hop), ins.at[which, chunk_rows(1, 0), own_cols],
-                    ins.at[which, chunk_rows(direction, hop), own_cols], along("z", direction * hop),
-                )
-    for which in range(2):
-        to_pair(which, 1, 0)
+    for steps in FIRST:
+        pass_on(0, steps)
+        pass_on(1, steps)
+    to_pair(0, 1, 0)
+    to_pair(1, 1, 0)
     own_half, other_half = (pl.ds(pl.multiple_of(i * HH, 128), HH) for i in (c, other))
     send(("w", 0), w_in.at[:, other_half], wi_pair.at[pl.ds(pl.multiple_of(c * W, 128), W)], pair)
     send(("w", 1), w_out.at[other_half], wo_pair.at[:, own_cols], pair)
 
-    for steps in (2, 1, 4, 3):
-        gather_step(steps)
+    own_weights = [
+        local(w_in.at[:, own_half], wi_pair.at[pl.ds(pl.multiple_of(c * W, 128), W)]),
+        local(w_out.at[own_half], wo_pair.at[:, own_cols]),
+    ]
+    last = []
+    chunk_in(0, 2)
+    pass_on(0, 4)
+    chunk_in(1, 2)
+    pass_on(1, 4)
+    pass_on(0, 3)
+    pass_on(1, 3)
+    share_in(0, 2)
+    share_in(1, 2)
+    chunk_in(0, 1)
+    share_in(0, 1)
+    chunk_in(1, 1)
+    share_in(1, 1)
+    chunk_in(0, 4)
+    pass_on(0, 6)
+    chunk_in(1, 4)
+    pass_on(1, 6)
+    pass_on(0, 5)
+    pass_on(1, 5)
+    share_in(0, 4)
+    share_in(1, 4)
+    chunk_in(0, 3)
+    share_in(0, 3)
+    chunk_in(1, 3)
+    share_in(1, 3)
     for copy in own_weights:
         copy.wait()
     arrived("w", 0)
     pair_has(0, 0)
     product(0, 0)
     scatter1(0, 0)
-    gather_step(6)
+    chunk_in(0, 6)
+    pass_on(0, 8)
+    chunk_in(1, 6)
+    pass_on(1, 8)
+    pass_on(0, 7)
+    pass_on(1, 7)
+    share_in(0, 6)
+    share_in(1, 6)
     arrived("w", 1)
+    full_weights = [local(w_in, wi), local(w_out, wo)]
     pair_has(1, 0)
     product(1, 0)
     scatter1(1, 0)
-    gather_step(5)
-    gather_step(8)
-    gather_step(7)
+    chunk_in(0, 5)
+    share_in(0, 5)
+    chunk_in(1, 5)
+    share_in(1, 5)
+    chunk_in(0, 8)
+    share_in(0, 8)
+    chunk_in(1, 8)
+    share_in(1, 8)
+    chunk_in(0, 7)
+    share_in(0, 7)
+    chunk_in(1, 7)
+    share_in(1, 7)
     scatter2(0, 0)
     pair_has(0, 1)
     product(0, 1)
@@ -313,45 +363,73 @@
     product(1, 1)
     scatter1(1, 1)
     finish(0, 0)
+    scatter2(0, 1)
     finish(1, 0)
-    scatter2(0, 1)
+    scatter2(1, 1)
+    finish(0, 1)
     gather2(0, 0)
-    scatter2(1, 1)
+    finish(1, 1)
+    gather2(0, 1)
     gather2(1, 0)
-    finish(0, 1)
-    finish(1, 1)
+    gather2(1, 1)
     gather3(0, 0)
-    gather2(0, 1)
-    gather2(1, 1)
-    gather3(1, 0)
+    for copy in full_weights:
+        copy.wait()
     project(0, 0)
     zraw(0, 0)
     gather3(0, 1)
+    project(0, 1)
+    zraw(0, 1)
+    last.append(weight_grad(0))
+    gather3(1, 0)
     project(1, 0)
     zraw(1, 0)
-    project(0, 1)
-    zraw(0, 1)
     gather3(1, 1)
+    zstep(0, 6)
     project(1, 1)
     zraw(1, 1)
-    zstep(0, 6)
+    sent()
     zstep(1, 6)
-    last = [weight_grad(0)]
-    zstep(0, 4)
-    zstep(1, 4)
+    zstep(0, 3)
     last.append(weight_grad(1))
-    zstep(0, 2)
-    zstep(1, 2)
+    zstep(1, 3)
+    sent()
     last.append(zend(0))
     last.append(zend(1))
-    for copy in copies.values():
-        copy.wait_send()
+    sent()
     for copy in last:
         copy.wait()
 
 
+def to_outputs(*refs):
+    sources, targets, held, sems = refs[:4], refs[4:8], refs[8:12], refs[12]
+    blocks = [(i, pl.ds(k * held[i].shape[0] // 4, held[i].shape[0] // 4)) for k in range(4) for i in (2, 3)]
+    blocks += [(0, pl.ds(0, CHUNK)), (1, pl.ds(0, CHUNK))]
+    first = [pltpu.make_async_copy(sources[i].at[r], held[i].at[r], sems.at[0, n]) for n, (i, r) in enumerate(blocks)]
+    second = [pltpu.make_async_copy(held[i].at[r], targets[i].at[r], sems.at[1, n]) for n, (i, r) in enumerate(blocks)]
+    for copy in first:
+        copy.start()
+    for before, after in zip(first, second):
+        before.wait()
+        after.start()
+    for copy in second:
+        copy.wait()
+
+
 def shards(tokens, cotangent, w_in, w_out):
-    copies = 2 * 15 + 2 * 16 + 2 + 4 * 6 * 4 + 4 * 8 + 2 * 15
+    results = kernel_call(tokens, cotangent, w_in, w_out)
+    return pl.pallas_call(
+        to_outputs,
+        out_shape=tuple(jax.ShapeDtypeStruct(r.shape, r.dtype) for r in results),
+        in_specs=[pl.BlockSpec(memory_space=pl.ANY)] * 4,
+        out_specs=(pl.BlockSpec(memory_space=pl.ANY),) * 4,
+        scratch_shapes=[*(pltpu.VMEM(r.shape, r.dtype) for r in results), pltpu.SemaphoreType.DMA((2, 10))],
+        name="to_outputs",
+    )(*results)
+
+
+def kernel_call(tokens, cotangent, w_in, w_out):
+    copies = 2 * 15 + 2 * 16 + 2 + 2 * GROUPS * 32 + 2 * 15
     anywhere = pl.BlockSpec(memory_space=pl.ANY)
     shape = jax.ShapeDtypeStruct
     return pl.pallas_call(
@@ -359,7 +437,7 @@
         out_shape=(
             shape((CHUNK, W), BF16), shape((CHUNK, W), BF16), shape((W, H), BF16), shape((H, W), BF16),
         ),
-        in_specs=[anywhere] * 4,
+        in_specs=[pl.BlockSpec(memory_space=pltpu.HBM)] * 4,
         out_specs=(anywhere,) * 4,
         scratch_shapes=[
             pltpu.VMEM((2, TOKENS, CW), BF16),
@@ -373,8 +451,8 @@
             pltpu.VMEM((2, GROUPS, 2, 3, PIECE, W), BF16),
             pltpu.VMEM((2, 2, TOKENS, HH), BF16),
             pltpu.VMEM((2, TOKENS, W), BF16),
-            pltpu.VMEM((2, 2, 4, 2, CHUNK, W), BF16),
-            pltpu.VMEM((2, 2, 3, CHUNK, W), BF16),
+            pltpu.VMEM((2, 2, 3, 3, CHUNK, W), BF16),
+            pltpu.VMEM((2, 2, 2, CHUNK, W), BF16),
             pltpu.VMEM((2, CHUNK, W), BF16),
             pltpu.VMEM((W, H), BF16),
             pltpu.VMEM((H, W), BF16),
@@ -383,7 +461,7 @@
             pltpu.SemaphoreType.DMA((copies,)),
         ],
         compiler_params=pltpu.CompilerParams(
-            collective_id=0, has_side_effects=True, vmem_limit_bytes=48 * 2**20
+            collective_id=0, has_side_effects=True, vmem_limit_bytes=60 * 2**20
         ),
         cost_estimate=pl.CostEstimate(flops=12 * TOKENS * W * H, bytes_accessed=10 * W * H, transcendentals=0),
         name="ffn",

time: 85.3 us -> 79.2 us (0.928)
  local copies, waits for them, and re-layouts: 7.25 us -> 0 us
    unnamed x12 -> x0, local copies, waits for them, and re-layouts: 7.25 us -> none
    pallas_call x1 -> x2, Pallas kernels: 77.1 us -> 77.8 us  [the longest x1 75.2 us: kernel_call(): pl.pallas_call(body, out_shape=(shape((CHUNK, W), BF16), shape((CHUNK, W)...]
where the time goes in v2:
time: 79.2 us; the launch traced here: 78.4 us
  Pallas kernels  77.8 us (98%)
    pallas_call x1, Pallas kernels, kernel_call(): pl.pallas_call(body, out_shape=(shape((CHUNK, W), BF16), shape((CHUNK, W)...  75.2 us
    pallas_call x1, Pallas kernels, shards(): pl.pallas_call(to_outputs, out_shape=tuple((jax.ShapeDtypeStruct(r.shape,...  2.54 us

profile of v2, /device:TPU:6, one launch (start us, length us, event | category | flops | bytes accessed | tf_op | source)
XLA Modules:
  0.0 78.4 jit_solution(4005420154353648069)
XLA Ops:
  0.6 75.2 %ffn.1 = (bf16[32,384]{1,0:T(8,128)(2,1)}, bf16[32,384]{1,0:T(8,128)(2,1)}, bf16[384,1536]{1,0:T(8,128)(2,1)}, bf16[1536,384]{1,0:T(8,128)(2,1)}) custom-call(bf16[32,384]{1,0:T(8,128)(2,1)} %tokens.1, bf16[32,384]{1,0:T(8,128)(2,1)} %cotangent.1, bf16[384,1536]{1,0:T(8,128)(2,1)} %w_in.1, bf16[1536,384]{1,0:T(8,128)(2,1)} %w_out.1), custom_call_target="tpu_custom_call" | custom-call | flops 3623878656 | bytes 5898240 | tf_op jit(solution)/shard_map/ffn/pallas_call | solution.py:435
  75.9 2.5 %to_outputs.1 = (bf16[32,384]{1,0:T(8,128)(2,1)}, bf16[32,384]{1,0:T(8,128)(2,1)}, bf16[384,1536]{1,0:T(8,128)(2,1)}, bf16[1536,384]{1,0:T(8,128)(2,1)}) custom-call(bf16[32,384]{1,0:T(8,128)(2,1)} %get-tuple-element.8.refs_0_, bf16[32,384]{1,0:T(8,128)(2,1)} %get-tuple-element.9.refs_1_, bf16[384,1536]{1,0:T(8,128)(2,1)} %get-tuple-element.10.refs_2_, ...), custom_call_target="tpu_custom_call" | custom-call | tf_op jit(solution)/shard_map/to_outputs/pallas_call | solution.py:421

commit v3 on v2

--- a/solution.py
+++ b/solution.py
@@ -105,35 +105,18 @@
                     ins.at[which, chunk_rows(direction, steps), own_cols], along("z", direction * hop),
                 )
 
-    def to_pair(which, direction, steps):
-        rows = chunk_rows(direction, steps)
-        key = ("pair", which, direction, steps)
-        send(key, ins.at[which, rows, own_cols], ins.at[which, rows, own_cols], pair)
-
     def chunk_in(which, *many):
         for steps in many:
             for direction in (1, -1):
                 if steps <= reach(which, direction):
                     arrived("gather", which, direction, steps)
 
-    def share_in(which, *many):
-        for steps in many:
-            for direction in (1, -1):
-                if steps <= reach(which, direction):
-                    to_pair(which, direction, steps)
-
-    def pair_has(which, group):
-        for place in range(SPAN * group, SPAN * group + SPAN):
-            slot = ORDER[place]
-            if slot == 0:
-                arrived("pair", which, 1, 0)
-            elif slot == 8:
-                arrived("pair", which, 1 if which == 0 else -1, 8)
-            else:
-                arrived("pair", which, *((-1, slot) if slot < 8 else (1, 16 - slot)))
-
     def group_rows(group, begin=0, count=ROWS):
         return pl.ds(group * ROWS + begin, count)
+
+    def to_pair(which, group):
+        place = (which, group_rows(group), own_cols)
+        send(("pair", which, group), ins.at[place], ins.at[place], pair)
 
     def product(which, group):
         block = ins[which, group_rows(group), :]
@@ -213,20 +196,17 @@
             place = (which, c, part_at(group, at[first]), cols(half))
             for step in (2, 1, 3):
                 send(("g2", which, group, half, step), full.at[place], full.at[place], along(first, step))
-            send(("gp", which, group, half, 0), full.at[place], full.at[place], pair)
 
     def gather3(which, group):
-        for step in (1, 3, 2):
-            for half in range(2):
-                first = axes(half)[0]
+        for half in range(2):
+            for step in (1, 3, 2):
                 arrived("g2", which, group, half, step)
-                place = (which, c, part_at(group, (at[first] + 4 - step) % 4), cols(half))
-                send(("gp", which, group, half, step), full.at[place], full.at[place], pair)
+            place = (which, c, group_rows(group), cols(half))
+            send(("gp", which, group, half), full.at[place], full.at[place], pair)
 
     def project(which, group):
         for half in range(2):
-            for step in range(4):
-                arrived("gp", which, group, half, step)
+            arrived("gp", which, group, half)
         value = None
         for k in range(2):
             block = full[which, k, group_rows(group), :]
@@ -288,11 +268,7 @@
     for steps in FIRST:
         pass_on(0, steps)
         pass_on(1, steps)
-    to_pair(0, 1, 0)
-    to_pair(1, 1, 0)
     own_half, other_half = (pl.ds(pl.multiple_of(i * HH, 128), HH) for i in (c, other))
-    send(("w", 0), w_in.at[:, other_half], wi_pair.at[pl.ds(pl.multiple_of(c * W, 128), W)], pair)
-    send(("w", 1), w_out.at[other_half], wo_pair.at[:, own_cols], pair)
 
     own_weights = [
         local(w_in.at[:, own_half], wi_pair.at[pl.ds(pl.multiple_of(c * W, 128), W)]),
@@ -305,28 +281,24 @@
     pass_on(1, 4)
     pass_on(0, 3)
     pass_on(1, 3)
-    share_in(0, 2)
-    share_in(1, 2)
+    send(("w", 0), w_in.at[:, other_half], wi_pair.at[pl.ds(pl.multiple_of(c * W, 128), W)], pair)
+    send(("w", 1), w_out.at[other_half], wo_pair.at[:, own_cols], pair)
     chunk_in(0, 1)
-    share_in(0, 1)
     chunk_in(1, 1)
-    share_in(1, 1)
     chunk_in(0, 4)
     pass_on(0, 6)
     chunk_in(1, 4)
     pass_on(1, 6)
     pass_on(0, 5)
     pass_on(1, 5)
-    share_in(0, 4)
-    share_in(1, 4)
     chunk_in(0, 3)
-    share_in(0, 3)
+    to_pair(0, 0)
     chunk_in(1, 3)
-    share_in(1, 3)
+    to_pair(1, 0)
     for copy in own_weights:
         copy.wait()
     arrived("w", 0)
-    pair_has(0, 0)
+    arrived("pair", 0, 0)
     product(0, 0)
     scatter1(0, 0)
     chunk_in(0, 6)
@@ -335,31 +307,25 @@
     pass_on(1, 8)
     pass_on(0, 7)
     pass_on(1, 7)
-    share_in(0, 6)
-    share_in(1, 6)
     arrived("w", 1)
     full_weights = [local(w_in, wi), local(w_out, wo)]
-    pair_has(1, 0)
+    arrived("pair", 1, 0)
     product(1, 0)
     scatter1(1, 0)
     chunk_in(0, 5)
-    share_in(0, 5)
     chunk_in(1, 5)
-    share_in(1, 5)
     chunk_in(0, 8)
-    share_in(0, 8)
     chunk_in(1, 8)
-    share_in(1, 8)
     chunk_in(0, 7)
-    share_in(0, 7)
+    to_pair(0, 1)
     chunk_in(1, 7)
-    share_in(1, 7)
+    to_pair(1, 1)
     scatter2(0, 0)
-    pair_has(0, 1)
+    arrived("pair", 0, 1)
     product(0, 1)
     scatter1(0, 1)
     scatter2(1, 0)
-    pair_has(1, 1)
+    arrived("pair", 1, 1)
     product(1, 1)
     scatter1(1, 1)
     finish(0, 0)
@@ -388,12 +354,11 @@
     zstep(0, 6)
     project(1, 1)
     zraw(1, 1)
-    sent()
     zstep(1, 6)
     zstep(0, 3)
+    sent()
+    zstep(1, 3)
     last.append(weight_grad(1))
-    zstep(1, 3)
-    sent()
     last.append(zend(0))
     last.append(zend(1))
     sent()
@@ -429,7 +394,7 @@
 
 
 def kernel_call(tokens, cotangent, w_in, w_out):
-    copies = 2 * 15 + 2 * 16 + 2 + 2 * GROUPS * 32 + 2 * 15
+    copies = 2 * 15 + 2 * GROUPS + 2 + 2 * GROUPS * 26 + 2 * 15
     anywhere = pl.BlockSpec(memory_space=pl.ANY)
     shape = jax.ShapeDtypeStruct
     return pl.pallas_call(

time: 79.2 us -> 78 us (0.985)
  Pallas kernels: 77.8 us -> 76.1 us
    pallas_call x1, Pallas kernels: 75.2 us -> 73.6 us  [kernel_call(): pl.pallas_call(body, out_shape=(shape((CHUNK, W), BF16), shape((CHUNK, W)...]
where the time goes in v3:
time: 78 us; the launch traced here: 76.8 us
  Pallas kernels  76.1 us (98%)
    pallas_call x1, Pallas kernels, kernel_call(): pl.pallas_call(body, out_shape=(shape((CHUNK, W), BF16), shape((CHUNK, W)...  73.6 us
    pallas_call x1, Pallas kernels, shards(): pl.pallas_call(to_outputs, out_shape=tuple((jax.ShapeDtypeStruct(r.shape,...  2.54 us

profile of v3, /device:TPU:6, one launch (start us, length us, event | category | flops | bytes accessed | tf_op | source)
XLA Modules:
  0.0 76.8 jit_solution(8384505052798026001)
XLA Ops:
  0.6 73.6 %ffn.1 = (bf16[32,384]{1,0:T(8,128)(2,1)}, bf16[32,384]{1,0:T(8,128)(2,1)}, bf16[384,1536]{1,0:T(8,128)(2,1)}, bf16[1536,384]{1,0:T(8,128)(2,1)}) custom-call(bf16[32,384]{1,0:T(8,128)(2,1)} %tokens.1, bf16[32,384]{1,0:T(8,128)(2,1)} %cotangent.1, bf16[384,1536]{1,0:T(8,128)(2,1)} %w_in.1, bf16[1536,384]{1,0:T(8,128)(2,1)} %w_out.1), custom_call_target="tpu_custom_call" | custom-call | flops 3623878656 | bytes 5898240 | tf_op jit(solution)/shard_map/ffn/pallas_call | solution.py:400
  74.2 2.5 %to_outputs.1 = (bf16[32,384]{1,0:T(8,128)(2,1)}, bf16[32,384]{1,0:T(8,128)(2,1)}, bf16[384,1536]{1,0:T(8,128)(2,1)}, bf16[1536,384]{1,0:T(8,128)(2,1)}) custom-call(bf16[32,384]{1,0:T(8,128)(2,1)} %get-tuple-element.8.refs_0_, bf16[32,384]{1,0:T(8,128)(2,1)} %get-tuple-element.9.refs_1_, bf16[384,1536]{1,0:T(8,128)(2,1)} %get-tuple-element.10.refs_2_, ...), custom_call_target="tpu_custom_call" | custom-call | tf_op jit(solution)/shard_map/to_outputs/pallas_call | solution.py:386

commit v4 on v3

--- a/solution.py
+++ b/solution.py
@@ -295,18 +295,18 @@
     to_pair(0, 0)
     chunk_in(1, 3)
     to_pair(1, 0)
+    chunk_in(0, 6)
+    pass_on(0, 8)
+    chunk_in(1, 6)
+    pass_on(1, 8)
+    pass_on(0, 7)
+    pass_on(1, 7)
     for copy in own_weights:
         copy.wait()
     arrived("w", 0)
     arrived("pair", 0, 0)
     product(0, 0)
     scatter1(0, 0)
-    chunk_in(0, 6)
-    pass_on(0, 8)
-    chunk_in(1, 6)
-    pass_on(1, 8)
-    pass_on(0, 7)
-    pass_on(1, 7)
     arrived("w", 1)
     full_weights = [local(w_in, wi), local(w_out, wo)]
     arrived("pair", 1, 0)

time: 78 us -> 79 us (1.013); the launches traced: 76.8 us -> 78.7 us
  Pallas kernels: 76.1 us -> 78.1 us
    pallas_call x1, Pallas kernels: 73.6 us -> 75.5 us  [kernel_call(): pl.pallas_call(body, out_shape=(shape((CHUNK, W), BF16), shape((CHUNK, W)...]
where the time goes in v4:
time: 79 us; the launch traced here: 78.7 us
  Pallas kernels  78.1 us (99%)
    pallas_call x1, Pallas kernels, kernel_call(): pl.pallas_call(body, out_shape=(shape((CHUNK, W), BF16), shape((CHUNK, W)...  75.5 us
    pallas_call x1, Pallas kernels, shards(): pl.pallas_call(to_outputs, out_shape=tuple((jax.ShapeDtypeStruct(r.shape,...  2.54 us

profile of v4, /device:TPU:6, one launch (start us, length us, event | category | flops | bytes accessed | tf_op | source)
XLA Modules:
  0.0 78.7 jit_solution(3542086711483330392)
XLA Ops:
  0.6 75.5 %ffn.1 = (bf16[32,384]{1,0:T(8,128)(2,1)}, bf16[32,384]{1,0:T(8,128)(2,1)}, bf16[384,1536]{1,0:T(8,128)(2,1)}, bf16[1536,384]{1,0:T(8,128)(2,1)}) custom-call(bf16[32,384]{1,0:T(8,128)(2,1)} %tokens.1, bf16[32,384]{1,0:T(8,128)(2,1)} %cotangent.1, bf16[384,1536]{1,0:T(8,128)(2,1)} %w_in.1, bf16[1536,384]{1,0:T(8,128)(2,1)} %w_out.1), custom_call_target="tpu_custom_call" | custom-call | flops 3623878656 | bytes 5898240 | tf_op jit(solution)/shard_map/ffn/pallas_call | solution.py:400
  76.2 2.5 %to_outputs.1 = (bf16[32,384]{1,0:T(8,128)(2,1)}, bf16[32,384]{1,0:T(8,128)(2,1)}, bf16[384,1536]{1,0:T(8,128)(2,1)}, bf16[1536,384]{1,0:T(8,128)(2,1)}) custom-call(bf16[32,384]{1,0:T(8,128)(2,1)} %get-tuple-element.8.refs_0_, bf16[32,384]{1,0:T(8,128)(2,1)} %get-tuple-element.9.refs_1_, bf16[384,1536]{1,0:T(8,128)(2,1)} %get-tuple-element.10.refs_2_, ...), custom_call_target="tpu_custom_call" | custom-call | tf_op jit(solution)/shard_map/to_outputs/pallas_call | solution.py:386
